TPU v7x, 256 devices: a whole 4x4x8 slice. The times are simulated.
256 devices in a mesh: tm: 32 (over y_lo, z, core), stn: 8 (over x, y_hi).
Axes of the slice: x: 4, y: 4 (y_hi: 2, y_lo: 2; y = y_hi * 2 + y_lo), z: 8, core: 2. Of those that a mesh axis runs over, the one named last changes fastest.
Arguments:
- voltages: bfloat16 [1024, 262144], P('stn', 'tm'), may hold values from -12 to 12, as said below
- fir_taps: float32 [12, 512], replicated, may hold values from -0.02 to 0.02
Outputs:
- visibilities: float32 [256, 2, 1024, 1024], P('tm', None, 'stn')
Inputs may be any that keep to these rules, and one draw needn't show every extreme that they name: `voltages`: whole numbers. Each input holds a common sky signal, delayed by up to 64 samples, plus its own noise.
All inputs are finite; a program needn't handle non-finite values.
Results may differ from a plain program's by a relative error of at most 0.0022.
Values may be sent and summed in bfloat16 or wider, within the bound.
A program may use at most 128 MiB of HBM per device.

v0:
```python
import math

import jax
import jax.numpy as jnp
from jax import lax
from jax.sharding import PartitionSpec as P


def passed_along(value, axis, steps):
    count = lax.axis_size(axis)
    initial, last = (max(0, -steps), min(count, count - steps))
    return lax.ppermute(value, axis, [(source, source + steps) for source in range(initial, last)])


def conjugate_pair(spectra_part):
    swapped = jnp.stack([spectra_part[1], -spectra_part[0]], axis=0)
    return jnp.stack([spectra_part, swapped], axis=0)


def gram_product(left_pair, right_part):
    return jnp.einsum("qptcr,ptcs->cqrs", left_pair, right_part, preferred_element_type=jnp.float32)


def per_device(voltages, fir_taps):
    row_count = voltages.shape[0]
    tap_count = fir_taps.shape[0]
    frame_len = fir_taps.shape[1]
    frames_dev = voltages.shape[1] // frame_len
    channels = frame_len // 2
    framed = voltages.reshape(row_count, frames_dev, frame_len)
    samples = framed.astype(jnp.float32)
    margin = jnp.zeros((row_count, tap_count - 1, frame_len), jnp.float32)
    padded = jnp.concatenate([margin, samples, margin], axis=1)
    span_frames = frames_dev + tap_count - 1
    filtered = jnp.zeros((row_count, span_frames, frame_len), jnp.float32)
    for tap_index in range(tap_count):
        first_frame = tap_count - 1 - tap_index
        filtered = (
            filtered + fir_taps[tap_index] * padded[:, first_frame : first_frame + span_frames]
        )
    tail_sums = filtered[:, frames_dev:]
    received = passed_along(tail_sums, "tm", 1)
    rest_zero = jnp.zeros((row_count, frames_dev - tap_count + 1, frame_len), jnp.float32)
    own_frames = filtered[:, :frames_dev] + jnp.concatenate([received, rest_zero], axis=1)
    channel_ids = lax.broadcasted_iota(jnp.int32, (channels, frame_len), 0)
    sample_ids = lax.broadcasted_iota(jnp.int32, (channels, frame_len), 1)
    phase_index = channel_ids * sample_ids % frame_len
    angle_grid = phase_index.astype(jnp.float32) * (2.0 * math.pi / frame_len)
    dft_table = jnp.stack([jnp.cos(angle_grid), -jnp.sin(angle_grid)], axis=0)
    spectrum = jnp.einsum(
        "rtn,pcn->ptcr",
        own_frames,
        dft_table,
        precision=lax.Precision.HIGHEST,
        preferred_element_type=jnp.float32,
    ).astype(jnp.bfloat16)
    turned = lax.all_to_all(spectrum, "tm", split_axis=2, concat_axis=1, tiled=True)
    frames_all = turned.shape[1]
    local_pair = conjugate_pair(turned)
    gram_part = gram_product(local_pair, lax.all_gather(turned, "stn", axis=3, tiled=True))
    return gram_part / frames_all


def solution(mesh):
    placed = (P("stn", "tm"), P())
    return jax.shard_map(
        per_device,
        mesh=mesh,
        in_specs=placed,
        out_specs=P("tm", None, "stn", None),
        check_vma=False,
    )
```

profile of v0, /device:TPU:1, one launch (start us, length us, event | category | flops | bytes accessed | tf_op | source)
XLA Modules:
  0.0 389.6 jit_solution(11798330302977107601)
XLA Ops:
  6.5 1.0 fusion.39
  7.6 2.0 convert_element_type.33
  9.6 2.7 copy.46
  12.2 0.3 broadcast_in_dim.4
  12.6 7.8 %pad_maximum_fusion = f32[128,38,512]{2,0,1:T(8,128)} fusion(f32[128,11,512]{2,0,1:T(8,128)S(1)} %broadcast_in_dim.4, f32[128,16,512]{2,0,1:T(8,128)} %bitcast.51), kind=kLoop, calls=%fused_computation.2 | loop fusion | flops 4980736 | bytes 17039360 | tf_op jit(solution)/shard_map/concatenate | solution.py:33
  20.4 29.8 %fusion.3 = f32[128,27,512]{2,0,1:T(8,128)S(1)} fusion(f32[128,38,512]{2,0,1:T(8,128)} %pad_maximum_fusion, f32[128,16,512]{2,0,1:T(8,128)} %bitcast.52, f32[512]{0:T(512)S(1)} %bitcast.71, f32[512]{0:T(512)S(1)} %bitcast.72, f32[512]{0:T(512)S(1)} %bitcast.62, f32[512]{0:T(512)S(1)} %bitcast.63, f32[512]{0:T(512)S(1)} %bitcast.64, f32[512]{0:T(512)S(1)} %bitcast.65, ...), kind=kLoop, calls=%fused_computation.6 | loop fusion | flops 40697856 | bytes 82075648 | tf_op jit(solution)/shard_map/add | solution.py:39
  50.3 0.3 slice.124
  50.6 5.1 %collective-permute-start = (f32[128,11,512]{2,0,1:T(8,128)S(1)}, f32[128,11,512]{2,0,1:T(8,128)S(1)}, u32[]{:S(2)}, u32[]{:S(2)}) collective-permute-start(f32[128,11,512]{2,0,1:T(8,128)S(1)} %slice.124), channel_id=1, source_target_pairs={{0,8},{8,16},{16,24},{24,32},{32,40},{40,48},{48,56},{56,64},{64,7... | collective-permute-start | bytes 8650760 | tf_op jit(solution)/shard_map/ppermute | solution.py:12
  55.7 2.1 sine_negate_fusion
  57.7 29.1 %collective-permute-done = f32[128,11,512]{2,0,1:T(8,128)S(1)} collective-permute-done((f32[128,11,512]{2,0,1:T(8,128)S(1)}, f32[128,11,512]{2,0,1:T(8,128)S(1)}, u32[]{:S(2)}, u32[]{:S(2)}) %collective-permute-start) | collective-permute-done | bytes 2883616 | tf_op jit(solution)/shard_map/ppermute | solution.py:12
  86.9 7.2 %convert_bitcast_fusion = bf16[2,16,256,128]{3,2,1,0:T(8,128)(2,1)S(1)} fusion(f32[128,27,512]{2,0,1:T(8,128)S(1)} %fusion.3, f32[128,11,512]{2,0,1:T(8,128)S(1)} %collective-permute-done, f32[1,256,512]{2,1,0:T(8,128)S(1)} %get-tuple-element.19, f32[1,256,512]{2,1,0:T(8,128)S(1)} %get-tuple-element.20), kind=kOutput, calls=%fused_computation.35 | convolution fusion | flops 6444810240 | bytes 10223616 | tf_op jit(solution)/shard_map/rtn,pcn->ptcr/dot_general | solution.py:50
  94.1 1.4 copy.29
  95.5 60.4 %all_to_all.18 = bf16[2,16,256,128]{3,1,0,2:T(8,128)(2,1)S(1)} all-to-all(bf16[2,16,256,128]{3,1,0,2:T(8,128)(2,1)S(1)} %copy.29), channel_id=1, replica_groups=mesh['tm'=32,'stn'=8] {'tm'}, dimensions={2} | all-to-all | bytes 4194304 | tf_op jit(solution)/shard_map/all_to_all | solution.py:57
  155.8 1.9 copy.37
  157.7 2.7 copy.31
  160.4 4.4 %copy.36 = bf16[1,2,512,8,128]{2,4,1,0,3:T(8,128)(2,1)} copy(bf16[1,2,512,8,128]{4,3,2,1,0:T(8,128)(2,1)} %bitcast.58) | data formatting | bytes 4194304 | tf_op jit(solution)/shard_map/stack | solution.py:17
  164.8 0.8 copy.47
  165.8 0.3 copy.32
  166.1 0.7 copy.34
  166.8 0.3 copy.33
  167.0 0.7 copy.35
  167.7 1.5 maximum_bitcast_fusion
  169.2 198.5 %all-gather.2.cloned.1.call-done = bf16[2,512,8,1024]{3,1,0,2:T(8,128)(2,1)} async-done(((bf16[2,512,8,128]{3,1,0,2:T(8,128)(2,1)}), bf16[2,512,8,1024]{3,1,0,2:T(8,128)(2,1)}) %all-gather.2.cloned.1.call-update) | async-done | bytes 16777232 | tf_op jit(solution)/shard_map/all_gather | solution.py:60
  367.7 15.0 %bitcast_multiply_fusion = f32[8,2,128,1024]{3,2,1,0:T(8,128)} fusion(bf16[2,512,8,1024]{3,1,0,2:T(8,128)(2,1)} %all-gather.2.cloned.1.call-done, bf16[1,2,512,8,128]{2,4,1,0,3:T(8,128)(2,1)} %maximum_bitcast_fusion, bf16[1,2,512,8,128]{2,4,1,0,3:T(8,128)(2,1)} %copy.36), kind=kOutput, calls=%fused_computation.3 | convolution fusion | flops 4299161600 | bytes 29360128 | tf_op jit(solution)/shard_map/qptcr,ptcs->cqrs/dot_general | solution.py:21
  (3 shorter events, 0.2 us)
Async XLA Ops:
  6.5 361.2 %all-gather.2.cloned.1.call-start = ((), (), s32[]{:S(2)}) async-start(), calls=%async_computation.1 | async-start | bytes 18874368 | tf_op jit(solution)/shard_map/all_gather | solution.py:60
  50.6 36.3 %collective-permute-start = (f32[128,11,512]{2,0,1:T(8,128)S(1)}, f32[128,11,512]{2,0,1:T(8,128)S(1)}, u32[]{:S(2)}, u32[]{:S(2)}) collective-permute-start(f32[128,11,512]{2,0,1:T(8,128)S(1)} %slice.124), channel_id=1, source_target_pairs={{0,8},{8,16},{16,24},{24,32},{32,40},{40,48},{48,56},{56,64},{64,7... | collective-permute-start | bytes 8650760 | tf_op jit(solution)/shard_map/ppermute | solution.py:12
Sparse Core Ops, SparseCore 0:
  157.9 209.8 all-gather.1
where the time goes:
time: 390 us
  waiting for transfers between devices  228 us (58%)
  blocking collectives  60.4 us (15%)
  other arithmetic  43.4 us (11%)
  matrix products  22.2 us (6%)
  local copies, waits for them, and re-layouts  17.3 us (4%)
  between operations  13.5 us (3%)
  starting transfers between devices  5.12 us (1%)
    all_gather x1, waiting for transfers between devices, per_device(): lax.all_gather(turned, 'stn', axis=3, tiled=True)  198 us
    all_to_all x1, blocking collectives, per_device(): lax.all_to_all(spectrum, 'tm', split_axis=2, concat_axis=1, tiled=True)  60.4 us
    add x1, other arithmetic, per_device(): filtered + fir_taps[tap_index] * padded[:, first_frame:first_frame + span...  29.8 us
    ppermute x1, waiting for transfers between devices, passed_along(): lax.ppermute(value, axis, [(source, source + steps) for source in range(i...  29.1 us
    dot_general x1, matrix products, gram_product(): jnp.einsum('qptcr,ptcs->cqrs', left_pair, right_part, preferred_element_t...  15 us
    concatenate x1, other arithmetic, per_device(): padded = jnp.concatenate([margin, samples, margin], axis=1)  7.83 us
  transfers between devices with their start and end apart: 2, of which 2 were waited for; matrix products, arithmetic and copies ran while one was open for 3% of the time, Pallas kernels for 0%

commit v1 on v0

v1 whole, which is shorter than its diff:
```python
import functools

import jax
import jax.numpy as jnp
import numpy as np
from jax import lax
from jax.experimental import pallas as pl
from jax.experimental.pallas import tpu as pltpu
from jax.sharding import PartitionSpec as P

BF16 = jnp.bfloat16
F32 = jnp.float32
MESH = pl.DeviceIdType.MESH

TM, STN = 32, 8
ROWS = 128
FRAMES = 16
FRAME = 512
HALF = FRAME // 2
TAPS = 12
HALO = TAPS - 1
PAIRS = FRAMES // 2
ALL_INPUTS = ROWS * STN
ALL_FRAMES = FRAMES * TM
COLS = 256
COL_STEPS = ALL_INPUTS // COLS
HALO_PARTS = [(10, 1), (8, 2), (6, 2), (4, 2), (2, 2), (0, 2)]
STN_STEPS = [(1, 0), (3, 0), (0, 1), (1, 1), (3, 1), (2, 0), (2, 1)]


def dft_tables():
    index = np.arange(HALF)
    tables = []
    for parity in range(2):
        channel = 2 * np.arange(HALF // 2) + parity
        phase = (channel[:, None] * index[None, :]) % FRAME
        angle = phase * (2.0 * np.pi / FRAME)
        full = np.concatenate([np.cos(angle), -np.sin(angle)], axis=0)
        high = full.astype(BF16)
        low = (full - high.astype(np.float64)).astype(BF16)
        tables.append(np.stack([high, low]))
    return np.stack(tables)


def split(value):
    high = value.astype(BF16)
    return high, (value - high.astype(F32)).astype(BF16)


def nt_dot(left, right):
    return lax.dot_general(left, right, (((1,), (1,)), ((), ())), preferred_element_type=F32)


def correlator(
    volt_ref, taps_ref, table_ref, out_ref,
    x_buf, tap_buf, fold_buf, wide_buf, send_buf, spec_buf, left_buf, vis_buf,
    local_sem, halo_send_sem, halo_recv_sem, spec_sem, vis_sem,
):
    tm = lax.axis_index("tm")
    stn = lax.axis_index("stn")
    y_lo, z, core = tm // 16, (tm // 2) % 8, tm % 2
    x, y_hi = stn // 2, stn % 2

    own = pltpu.make_async_copy(
        volt_ref, x_buf.at[:, pl.ds(HALO * FRAME, FRAMES * FRAME)], local_sem.at[0]
    )
    own.start()

    def halo_copy(part):
        first, count = HALO_PARTS[part]
        return pltpu.make_async_remote_copy(
            src_ref=volt_ref.at[:, pl.ds((FRAMES - HALO + first) * FRAME, count * FRAME)],
            dst_ref=x_buf.at[:, pl.ds(first * FRAME, count * FRAME)],
            send_sem=halo_send_sem.at[part],
            recv_sem=halo_recv_sem.at[part],
            device_id=(tm + 1, stn),
            device_id_type=MESH,
        )

    @pl.when(tm < TM - 1)
    def _():
        for part in range(len(HALO_PARTS)):
            halo_copy(part).start()

    @pl.when(tm == 0)
    def _():
        x_buf[:, : HALO * FRAME] = jnp.zeros((ROWS, HALO * FRAME), BF16)

    for tap in range(TAPS):
        tap_buf[tap] = jnp.broadcast_to(taps_ref[tap : tap + 1, :], (16, FRAME))
    own.wait()

    def fir_pair(pair):
        base = pl.multiple_of(pair * 2 * FRAME, FRAME)

        def row_step(row_index, carry):
            row = pl.multiple_of(row_index * 16, 16)
            for lane in (0, 128):
                sums = []
                for part in range(2):
                    at = lane + part * HALF
                    totals = [None, None]
                    for frame in range(TAPS + 1):
                        value = x_buf[
                            pl.ds(row, 16), pl.ds(pl.multiple_of(base + frame * FRAME + at, 128), 128)
                        ].astype(F32)
                        for which in range(2):
                            tap = HALO + which - frame
                            if 0 <= tap < TAPS:
                                term = tap_buf[tap, :, at : at + 128] * value
                                totals[which] = term if totals[which] is None else totals[which] + term
                    sums.append(totals)
                for which in range(2):
                    even = sums[0][which] + sums[1][which]
                    odd = sums[0][which] - sums[1][which]
                    for parity, folded in enumerate((even, odd)):
                        high, low = split(folded)
                        at_row = pl.multiple_of(which * ROWS + row, 16)
                        fold_buf[parity, 0, pl.ds(at_row, 16), lane : lane + 128] = high
                        fold_buf[parity, 1, pl.ds(at_row, 16), lane : lane + 128] = low
            return carry

        lax.fori_loop(0, ROWS // 16, row_step, 0)

    def dft_pair(pair):
        for parity in range(2):
            high, low = fold_buf[parity, 0], fold_buf[parity, 1]
            result = (
                nt_dot(table_ref[parity, 0], high)
                + nt_dot(table_ref[parity, 1], high)
                + nt_dot(table_ref[parity, 0], low)
            )
            for which in range(2):
                for part in range(2):
                    first = (2 * parity + part) * FRAMES + 2 * pair + which
                    wide_buf[pl.ds(first, HALF // 2, stride=4 * FRAMES), :] = result[
                        part * 128 : (part + 1) * 128, which * ROWS : (which + 1) * ROWS
                    ]

    def pair_step(step, carry):
        pair = PAIRS - 1 - step
        for part in range(len(HALO_PARTS)):

            @pl.when((pair == len(HALO_PARTS) - 1 - part) & (tm > 0))
            def _():
                halo_copy(part).wait_recv()

        fir_pair(pair)
        dft_pair(pair)
        return carry

    lax.fori_loop(0, PAIRS, pair_step, 0)

    def pack_step(step, carry):
        rows = wide_buf[pl.ds(pl.multiple_of(step * 256, 256), 256), :]
        send_buf[pl.ds(step * 8, 8)] = rows.reshape(8, 2, FRAMES, ROWS).astype(BF16)
        return carry

    lax.fori_loop(0, HALF // 8, pack_step, 0)

    own_place = spec_buf.at[tm, :, :, pl.ds(pl.multiple_of(stn * ROWS, ROWS), ROWS)]
    keep = pltpu.make_async_copy(send_buf.at[tm * STN + stn], own_place, local_sem.at[1])
    keep.start()

    def send_step(step, carry):
        near = (step % 8) // 2
        d_z = jnp.where(step % 8 == 0, 4, jnp.where(step % 2 == 0, near, (8 - near) % 8))
        rest = step // 8
        to_core, rest = rest // 16, rest % 16
        to_x, rest = (x + rest % 4) % 4, rest // 4
        to_y_lo, to_y_hi = (y_lo + rest // 2) % 2, (y_hi + rest % 2) % 2
        to_tm = (to_y_lo * 8 + (z + d_z) % 8) * 2 + to_core
        to_stn = to_x * 2 + to_y_hi

        @pl.when((to_tm != tm) | (to_stn != stn))
        def _():
            pltpu.make_async_remote_copy(
                src_ref=send_buf.at[to_tm * STN + to_stn],
                dst_ref=own_place,
                send_sem=spec_sem.at[0],
                recv_sem=spec_sem.at[1],
                device_id=(to_tm, to_stn),
                device_id_type=MESH,
            ).start()

        return carry

    lax.fori_loop(0, TM * STN, send_step, 0)
    keep.wait()
    others = send_buf.at[pl.ds(0, TM * STN - 1)]
    pltpu.make_async_copy(others, others, spec_sem.at[1]).wait()

    def left_step(block, carry):
        at = pl.ds(pl.multiple_of(block * ROWS, ROWS), ROWS)
        real = spec_buf[:, 0, :, at].reshape(ALL_FRAMES, ROWS).T
        imag = spec_buf[:, 1, :, at].reshape(ALL_FRAMES, ROWS).T
        left_buf[block, 0, :, :ALL_FRAMES] = real
        left_buf[block, 0, :, ALL_FRAMES:] = imag
        left_buf[block, 1, :, :ALL_FRAMES] = imag
        left_buf[block, 1, :, ALL_FRAMES:] = -real
        return carry

    lax.fori_loop(0, STN, left_step, 0)

    def vis_copy(col_step, to_stn):
        at = pl.ds(pl.multiple_of(col_step * COLS, COLS), COLS)
        return vis_buf.at[col_step, to_stn], out_ref.at[stn, :, :, at]

    def col_loop(col_step, carry):
        at = pl.ds(pl.multiple_of(col_step * COLS, COLS), COLS)
        real = spec_buf[:, 0, :, at].reshape(ALL_FRAMES, COLS)
        imag = spec_buf[:, 1, :, at].reshape(ALL_FRAMES, COLS)

        def block_step(block, inner):
            left = left_buf[block].reshape(2 * ROWS, 2 * ALL_FRAMES)
            total = jnp.dot(left[:, :ALL_FRAMES], real, preferred_element_type=F32)
            total += jnp.dot(left[:, ALL_FRAMES:], imag, preferred_element_type=F32)
            vis_buf[col_step, block] = (total * (1.0 / ALL_FRAMES)).astype(BF16).reshape(2, ROWS, COLS)
            return inner

        lax.fori_loop(0, STN, block_step, 0)
        source, place = vis_copy(col_step, stn)
        pltpu.make_async_copy(source, place, local_sem.at[2]).start()
        for d_x, d_y in STN_STEPS:
            to_stn = ((x + d_x) % 4) * 2 + (y_hi + d_y) % 2
            source, place = vis_copy(col_step, to_stn)
            pltpu.make_async_remote_copy(
                src_ref=source,
                dst_ref=place,
                send_sem=vis_sem.at[0],
                recv_sem=vis_sem.at[1],
                device_id=(tm, to_stn),
                device_id_type=MESH,
            ).start()
        return carry

    lax.fori_loop(0, COL_STEPS, col_loop, 0)

    pltpu.make_async_copy(out_ref.at[0], out_ref.at[0], local_sem.at[2]).wait()
    pltpu.make_async_copy(others, others, spec_sem.at[0]).wait()
    received = out_ref.at[pl.ds(0, STN - 1)]
    pltpu.make_async_copy(received, received, vis_sem.at[0]).wait()
    pltpu.make_async_copy(received, received, vis_sem.at[1]).wait()

    @pl.when(tm < TM - 1)
    def _():
        for part in range(len(HALO_PARTS)):
            halo_copy(part).wait_send()


def per_device(voltages, fir_taps):
    tables = jnp.asarray(dft_tables())
    any_spec = pl.BlockSpec(memory_space=pl.ANY)
    vmem_spec = pl.BlockSpec(memory_space=pltpu.VMEM)
    vis = pl.pallas_call(
        correlator,
        out_shape=jax.ShapeDtypeStruct((STN, 2, ROWS, ALL_INPUTS), BF16),
        in_specs=[any_spec, vmem_spec, vmem_spec],
        out_specs=any_spec,
        scratch_shapes=[
            pltpu.VMEM((ROWS, (FRAMES + HALO) * FRAME), BF16),
            pltpu.VMEM((TAPS, 16, FRAME), F32),
            pltpu.VMEM((2, 2, 2 * ROWS, HALF), BF16),
            pltpu.VMEM((2 * HALF * FRAMES, ROWS), F32),
            pltpu.VMEM((HALF, 2, FRAMES, ROWS), BF16),
            pltpu.VMEM((TM, 2, FRAMES, ALL_INPUTS), BF16),
            pltpu.VMEM((STN, 2, ROWS, 2 * ALL_FRAMES), BF16),
            pltpu.VMEM((COL_STEPS, STN, 2, ROWS, COLS), BF16),
            pltpu.SemaphoreType.DMA((3,)),
            pltpu.SemaphoreType.DMA((len(HALO_PARTS),)),
            pltpu.SemaphoreType.DMA((len(HALO_PARTS),)),
            pltpu.SemaphoreType.DMA((2,)),
            pltpu.SemaphoreType.DMA((2,)),
        ],
        compiler_params=pltpu.CompilerParams(has_side_effects=True, vmem_limit_bytes=48 << 20),
        name="correlator",
    )(voltages, fir_taps, tables)
    return vis.astype(F32)


def solution(mesh):
    return jax.shard_map(
        per_device,
        mesh=mesh,
        in_specs=(P("stn", "tm"), P()),
        out_specs=P("tm", None, "stn", None),
        check_vma=False,
    )
```

time: 390 us -> 136 us (0.35)
  waiting for transfers between devices: 228 us -> 0 us
  Pallas kernels: 0 us -> 125 us
  blocking collectives: 60.4 us -> 0 us
  other arithmetic: 43.4 us -> 6.65 us
  matrix products: 22.2 us -> 0 us
  local copies, waits for them, and re-layouts: 17.3 us -> 3.39 us
  between operations: 13.5 us -> 0.01 us
  starting transfers between devices: 5.12 us -> 0 us
    all_gather x1 -> x0, waiting for transfers between devices: 198 us -> none  [per_device(): lax.all_gather(turned, 'stn', axis=3, tiled=True)]
    pallas_call x0 -> x1, Pallas kernels: none -> 125 us  [per_device(): pl.pallas_call(correlator, out_shape=jax.ShapeDtypeStruct((STN, 2, ROWS,...]
    all_to_all x1 -> x0, blocking collectives: 60.4 us -> none  [per_device(): lax.all_to_all(spectrum, 'tm', split_axis=2, concat_axis=1, tiled=True)]
    add x1 -> x0, other arithmetic: 29.8 us -> none  [per_device(): filtered + fir_taps[tap_index] * padded[:, first_frame:first_frame + span...]
    ppermute x1 -> x0, waiting for transfers between devices: 29.1 us -> none  [passed_along(): lax.ppermute(value, axis, [(source, source + steps) for source in range(i...]
    dot_general x2 -> x0, matrix products: 22.2 us -> none  [the longest x1 15 us: gram_product(): jnp.einsum('qptcr,ptcs->cqrs', left_pair, right_part, preferred_element_t...]
    concatenate x1 -> x0, other arithmetic: 7.83 us -> none  [per_device(): padded = jnp.concatenate([margin, samples, margin], axis=1)]
    all_to_all x3 -> x0, local copies, waits for them, and re-layouts: 5.33 us -> none  [per_device(): lax.all_to_all(spectrum, 'tm', split_axis=2, concat_axis=1, tiled=True)]
  transfers between devices with their start and end apart: 2 -> 0, of which waited for: 2 -> 0; matrix products, arithmetic and copies ran while one was open for 3% -> 0% of each run, Pallas kernels for 0% -> 0%
where the time goes in v1:
time: 136 us; the launch traced here: 135 us
  Pallas kernels  125 us (92%)
  other arithmetic  6.65 us (5%)
  local copies, waits for them, and re-layouts  3.39 us (2%)
    pallas_call x1, Pallas kernels, per_device(): pl.pallas_call(correlator, out_shape=jax.ShapeDtypeStruct((STN, 2, ROWS,...  125 us
    convert_element_type x1, other arithmetic, per_device(): return vis.astype(F32)  6.65 us
    unnamed x6, local copies, waits for them, and re-layouts  3.39 us

profile of v1, /device:TPU:1, one launch (start us, length us, event | category | flops | bytes accessed | tf_op | source)
XLA Modules:
  0.0 135.4 jit_solution(5714252303588587169)
XLA Ops:
  0.0 0.0 copy-start
  0.0 1.6 %copy-done = bf16[128,8192]{1,0:T(8,128)(2,1)S(1)} copy-done((bf16[128,8192]{1,0:T(8,128)(2,1)S(1)}, bf16[128,8192]{1,0:T(8,128)(2,1)}, u32[]{:S(2)}) %copy-start) | copy-done | bytes 2097176
  1.6 0.0 copy-start.1
  1.6 1.0 copy-done.1
  2.6 0.0 copy-start.2
  2.6 0.8 copy-done.2
  3.4 125.3 %correlator.1 = bf16[8,2,128,1024]{3,2,1,0:T(8,128)(2,1)} custom-call(bf16[128,8192]{1,0:T(8,128)(2,1)S(1)} %copy-done, f32[12,512]{1,0:T(8,128)S(1)} %copy-done.2, bf16[2,2,256,256]{3,2,1,0:T(8,128)(2,1)S(1)} %copy-done.1), custom_call_target="tpu_custom_call" | custom-call | tf_op jit(solution)/shard_map/correlator/pallas_call | solution.py:255
  128.7 6.7 %convert_element_type.3 = f32[8,2,128,1024]{3,2,1,0:T(8,128)} convert(bf16[8,2,128,1024]{3,2,1,0:T(8,128)(2,1)} %correlator.1) | non-fusion elementwise | flops 2097152 | bytes 12582912 | tf_op jit(solution)/shard_map/convert_element_type | solution.py:278
Async XLA Ops:
  0.0 1.6 %copy-start = (bf16[128,8192]{1,0:T(8,128)(2,1)S(1)}, bf16[128,8192]{1,0:T(8,128)(2,1)}, u32[]{:S(2)}) copy-start(bf16[128,8192]{1,0:T(8,128)(2,1)} %volt_ref.1) | copy-start | bytes 6291460
  1.6 1.0 copy-start.1
  2.6 0.8 copy-start.2

commit v2 on v1

v2 whole, which is shorter than its diff:
```python
import functools

import jax
import jax.numpy as jnp
import numpy as np
from jax import lax
from jax.experimental import pallas as pl
from jax.experimental.pallas import tpu as pltpu
from jax.sharding import PartitionSpec as P

BF16 = jnp.bfloat16
F32 = jnp.float32
MESH = pl.DeviceIdType.MESH

TM, STN = 32, 8
ROWS = 128
FRAMES = 16
FRAME = 512
HALF = FRAME // 2
TAPS = 12
HALO = TAPS - 1
QUAD = 4
QUADS = FRAMES // QUAD
ALL_INPUTS = ROWS * STN
ALL_FRAMES = FRAMES * TM
SLOTS = HALF // 2
PLANES = SLOTS // 8
COLS = 256
COL_STEPS = ALL_INPUTS // COLS
BLOCKS = 4
AFTER = QUAD
BEFORE = HALO - AFTER
SPAN = BEFORE + FRAMES + AFTER
STN_STEPS = [(1, 0), (3, 0), (0, 1), (1, 1), (3, 1), (2, 0), (2, 1), (0, 0)]


def dft_tables():
    index = np.arange(HALF)
    tables = []
    for parity in range(2):
        y_lo, y_hi, x, z = np.indices((2, 2, 4, 8)).reshape(4, -1)
        channel = 16 * (8 * y_lo + z) + 8 * y_hi + 2 * x + parity
        phase = (channel[:, None] * index[None, :]) % FRAME
        angle = phase * (2.0 * np.pi / FRAME)
        full = np.concatenate([np.cos(angle), -np.sin(angle)], axis=0)
        high = full.astype(BF16)
        low = (full - high.astype(np.float64)).astype(BF16)
        tables.append(np.stack([high, low]))
    return np.stack(tables)


def split(value):
    high = value.astype(BF16)
    return high, (value - high.astype(F32)).astype(BF16)


def nt_dot(left, right):
    return lax.dot_general(left, right, (((1,), (1,)), ((), ())), preferred_element_type=F32)


def correlator(
    volt_ref, taps_ref, table_ref, out_ref,
    x_buf, tap_buf, fold_buf, wide_buf, send_buf, spec_buf, left_buf, vis_buf,
    local_sem, halo_send_sem, halo_recv_sem, spec_sem, vis_sem,
):
    tm = lax.axis_index("tm")
    stn = lax.axis_index("stn")
    y_lo, z, core = tm >> 4, (tm >> 1) & 7, tm & 1
    x, y_hi = stn >> 1, stn & 1

    own = pltpu.make_async_copy(
        volt_ref, x_buf.at[:, pl.ds(BEFORE * FRAME, FRAMES * FRAME)], local_sem.at[0]
    )
    own.start()

    barrier = pltpu.get_barrier_semaphore()

    def greet(step, carry):
        for to_stn in range(STN):

            def signal():
                pl.semaphore_signal(
                    barrier, inc=1, device_id=(tm ^ step, stn ^ to_stn), device_id_type=MESH
                )

            if to_stn:
                signal()
            else:
                pl.when(step > 0)(signal)
        return carry

    lax.fori_loop(0, TM, greet, 0)

    def halo_copy(part):
        source, place, count, to_tm = (
            (FRAMES - BEFORE, 0, QUAD, tm + 1),
            (FRAMES - BEFORE + QUAD, QUAD, BEFORE - QUAD, tm + 1),
            (0, BEFORE + FRAMES, AFTER, (tm - 1) & (TM - 1)),
        )[part]
        return pltpu.make_async_remote_copy(
            src_ref=volt_ref.at[:, pl.ds(source * FRAME, count * FRAME)],
            dst_ref=x_buf.at[:, pl.ds(place * FRAME, count * FRAME)],
            send_sem=halo_send_sem.at[part],
            recv_sem=halo_recv_sem.at[part],
            device_id=(to_tm, stn),
            device_id_type=MESH,
        )

    pl.semaphore_wait(barrier, TM * STN - 1)

    def start_before():
        @pl.when(tm < TM - 1)
        def _():
            halo_copy(1).start()
            halo_copy(0).start()

    @pl.when(core == 0)
    def _():
        start_before()
        halo_copy(2).start()

    @pl.when(core == 1)
    def _():
        halo_copy(2).start()
        start_before()

    for tap in range(TAPS):
        tap_buf[tap] = jnp.broadcast_to(taps_ref[tap : tap + 1, :], (16, FRAME))
    own.wait()

    def fir(quad):
        base = quad * QUAD * FRAME

        def row_step(row_index, carry):
            row = pl.multiple_of(row_index * 16, 16)
            for lane in (0, 128):
                sums = []
                for part in range(2):
                    at = lane + part * HALF
                    totals = [None] * QUAD
                    for frame in range(HALO + QUAD):
                        first = pl.multiple_of(base + frame * FRAME + at, 128)
                        value = x_buf[pl.ds(row, 16), pl.ds(first, 128)].astype(F32)
                        for which in range(QUAD):
                            tap = HALO + which - frame
                            if 0 <= tap < TAPS:
                                term = tap_buf[tap, :, at : at + 128] * value
                                totals[which] = term if totals[which] is None else totals[which] + term
                    sums.append(totals)
                for which in range(QUAD):
                    even = sums[0][which] + sums[1][which]
                    odd = sums[0][which] - sums[1][which]
                    rows = pl.ds(pl.multiple_of((quad * QUAD + which) * ROWS + row, 16), 16)
                    for parity, folded in enumerate((even, odd)):
                        high, low = split(folded)
                        fold_buf[parity, 0, rows, lane : lane + 128] = high
                        fold_buf[parity, 1, rows, lane : lane + 128] = low
            return carry

        lax.fori_loop(0, ROWS // 16, row_step, 0)

    def dft(quad, parity):
        rows = pl.ds(pl.multiple_of(quad * QUAD * ROWS, QUAD * ROWS), QUAD * ROWS)
        high, low = fold_buf[parity, 0, rows], fold_buf[parity, 1, rows]
        result = (
            nt_dot(table_ref[parity, 0], high)
            + nt_dot(table_ref[parity, 1], high)
            + nt_dot(table_ref[parity, 0], low)
        )
        for which in range(QUAD):
            for part in range(2):
                first = part * FRAMES + QUAD * quad + which
                wide_buf[parity, pl.ds(first, SLOTS, stride=2 * FRAMES), :] = result[
                    part * SLOTS : (part + 1) * SLOTS, which * ROWS : (which + 1) * ROWS
                ]

    quads = [2, jnp.where(core == 0, 3, 1), jnp.where(core == 0, 1, 0), jnp.where(core == 0, 0, 3)]
    @pl.when(tm == 0)
    def _():
        x_buf[:, : BEFORE * FRAME] = jnp.zeros((ROWS, BEFORE * FRAME), BF16)

    def wait_halo(quad):
        for part in range(2):

            @pl.when((quad == part) & (tm > 0))
            def _():
                halo_copy(part).wait_recv()

        @pl.when(quad == 3)
        def _():
            halo_copy(2).wait_recv()

        @pl.when((quad == 3) & (tm == TM - 1))
        def _():
            x_buf[:, 3 * QUAD * FRAME : (3 * QUAD + HALO) * FRAME] = jnp.zeros((ROWS, HALO * FRAME), BF16)

    for step in range(QUADS):
        if step > 0:
            wait_halo(quads[step])
        fir(quads[step])
        dft(quads[step], 0)
        if step < QUADS - 1:
            dft(quads[step], 1)

    own_place = spec_buf.at[tm, :, :, pl.ds(pl.multiple_of(stn * ROWS, ROWS), ROWS)]
    def send(parity):
        def plane_step(step, carry):
            to_x, to_y_hi, to_y_lo = x ^ (step & 3), y_hi ^ ((step >> 2) & 1), y_lo ^ (step >> 3)
            to_stn = to_x * 2 + to_y_hi
            plane = (to_y_lo * 2 + to_y_hi) * 4 + to_x
            rows = wide_buf[parity, pl.ds(pl.multiple_of(plane * 256, 256), 256), :]
            send_buf[parity, plane] = rows.reshape(8, 2, FRAMES, ROWS).astype(BF16)
            for d_z in (4, 1, 7, 2, 6, 3, 5, 0):
                to_z = (z + d_z) & 7
                source = send_buf.at[parity, plane, to_z]

                def start():
                    pltpu.make_async_remote_copy(
                        src_ref=source,
                        dst_ref=own_place,
                        send_sem=spec_sem.at[0],
                        recv_sem=spec_sem.at[1],
                        device_id=(to_y_lo * 16 + to_z * 2 + 1 - parity, to_stn),
                        device_id_type=MESH,
                    ).start()

                if d_z:
                    start()
                else:
                    pl.when((step > 0) | (core == parity))(start)

                    @pl.when((step == 0) & (core != parity))
                    def _():
                        pltpu.make_async_copy(source, own_place, spec_sem.at[1]).start()

            return carry

        lax.fori_loop(0, PLANES, plane_step, 0)

    send(0)
    dft(quads[-1], 1)
    send(1)

    everything = spec_buf.at[:, :, :, :]
    pltpu.make_async_copy(everything, everything, spec_sem.at[1]).wait()

    def left_step(block, carry):
        at = pl.ds(pl.multiple_of(block * ROWS, ROWS), ROWS)
        real = spec_buf[:, 0, :, at].reshape(ALL_FRAMES, ROWS).T
        imag = spec_buf[:, 1, :, at].reshape(ALL_FRAMES, ROWS).T
        left_buf[block, 0, :, :ALL_FRAMES] = real
        left_buf[block, 0, :, ALL_FRAMES:] = imag
        left_buf[block, 1, :, :ALL_FRAMES] = imag
        left_buf[block, 1, :, ALL_FRAMES:] = -real
        return carry

    lax.fori_loop(0, STN, left_step, 0)

    to_tm = (tm >> 1) * 2 + y_hi
    out_channel = x * 2 + 1 - core

    def col_loop(col_step, carry):
        at = pl.ds(pl.multiple_of(col_step * COLS, COLS), COLS)
        real = spec_buf[:, 0, :, at].reshape(ALL_FRAMES, COLS)
        imag = spec_buf[:, 1, :, at].reshape(ALL_FRAMES, COLS)

        def block_step(step, inner):
            blocks = pl.ds(step * BLOCKS, BLOCKS)
            left = left_buf[blocks].reshape(BLOCKS * 2 * ROWS, 2 * ALL_FRAMES)
            total = jnp.dot(left[:, :ALL_FRAMES], real, preferred_element_type=F32)
            total += jnp.dot(left[:, ALL_FRAMES:], imag, preferred_element_type=F32)
            total = (total * (1.0 / ALL_FRAMES)).astype(BF16)
            vis_buf[col_step, blocks] = total.reshape(BLOCKS, 2, ROWS, COLS)
            return inner

        lax.fori_loop(0, STN // BLOCKS, block_step, 0)
        place = out_ref.at[out_channel, :, :, at]
        for d_x, d_y in STN_STEPS:
            to_stn = ((x + d_x) & 3) * 2 + (y_hi ^ d_y)

            def start():
                pltpu.make_async_remote_copy(
                    src_ref=vis_buf.at[col_step, to_stn],
                    dst_ref=place,
                    send_sem=vis_sem.at[0],
                    recv_sem=vis_sem.at[1],
                    device_id=(to_tm, to_stn),
                    device_id_type=MESH,
                ).start()

            if d_x or d_y:
                start()
            else:
                pl.when(core != y_hi)(start)

        @pl.when(core == y_hi)
        def _():
            pltpu.make_async_copy(vis_buf.at[col_step, stn], place, vis_sem.at[1]).start()

        return carry

    lax.fori_loop(0, COL_STEPS, col_loop, 0)

    others = spec_buf.at[pl.ds(0, TM - 1)]
    pltpu.make_async_copy(others, others, spec_sem.at[0]).wait()
    rest = send_buf.at[0, 0, pl.ds(0, STN - 1)]
    pltpu.make_async_copy(rest, rest, spec_sem.at[0]).wait()
    sent = out_ref.at[pl.ds(0, STN - 1)]
    pltpu.make_async_copy(sent, sent, vis_sem.at[0]).wait()

    @pl.when(core != y_hi)
    def _():
        pltpu.make_async_copy(out_ref.at[0], out_ref.at[0], vis_sem.at[0]).wait()

    pltpu.make_async_copy(out_ref, out_ref, vis_sem.at[1]).wait()

    @pl.when(tm < TM - 1)
    def _():
        halo_copy(0).wait_send()
        halo_copy(1).wait_send()

    halo_copy(2).wait_send()


def per_device(voltages, fir_taps):
    tables = jnp.asarray(dft_tables())
    any_spec = pl.BlockSpec(memory_space=pl.ANY)
    vmem_spec = pl.BlockSpec(memory_space=pltpu.VMEM)
    vis = pl.pallas_call(
        correlator,
        out_shape=pltpu.VMEM((STN, 2, ROWS, ALL_INPUTS), BF16),
        in_specs=[any_spec, vmem_spec, vmem_spec],
        out_specs=any_spec,
        scratch_shapes=[
            pltpu.VMEM((ROWS, SPAN * FRAME), BF16),
            pltpu.VMEM((TAPS, 16, FRAME), F32),
            pltpu.VMEM((2, 2, FRAMES * ROWS, HALF), BF16),
            pltpu.VMEM((2, SLOTS * 2 * FRAMES, ROWS), F32),
            pltpu.VMEM((2, PLANES, 8, 2, FRAMES, ROWS), BF16),
            pltpu.VMEM((TM, 2, FRAMES, ALL_INPUTS), BF16),
            pltpu.VMEM((STN, 2, ROWS, 2 * ALL_FRAMES), BF16),
            pltpu.VMEM((COL_STEPS, STN, 2, ROWS, COLS), BF16),
            pltpu.SemaphoreType.DMA((1,)),
            pltpu.SemaphoreType.DMA((3,)),
            pltpu.SemaphoreType.DMA((3,)),
            pltpu.SemaphoreType.DMA((2,)),
            pltpu.SemaphoreType.DMA((2,)),
        ],
        compiler_params=pltpu.CompilerParams(
            collective_id=0, has_side_effects=True, vmem_limit_bytes=56 << 20
        ),
        name="correlator",
    )(voltages, fir_taps, tables)
    return vis.astype(F32)


def solution(mesh):
    return jax.shard_map(
        per_device,
        mesh=mesh,
        in_specs=(P("stn", "tm"), P()),
        out_specs=P("tm", None, "stn", None),
        check_vma=False,
    )
```

time: 136 us -> 119 us (0.88)
  Pallas kernels: 125 us -> 114 us
  local copies, waits for them, and re-layouts: 3.39 us -> 0 us
  other arithmetic: 6.65 us -> 4.46 us
    pallas_call x1, Pallas kernels: 125 us -> 114 us  [per_device(): pl.pallas_call(correlator, out_shape=pltpu.VMEM((STN, 2, ROWS, ALL_INPUTS...]
    unnamed x6 -> x0, local copies, waits for them, and re-layouts: 3.39 us -> none
    convert_element_type x1, other arithmetic: 6.65 us -> 4.46 us  [per_device(): return vis.astype(F32)]
where the time goes in v2:
time: 119 us
  Pallas kernels  114 us (96%)
  other arithmetic  4.46 us (4%)
    pallas_call x1, Pallas kernels, per_device(): pl.pallas_call(correlator, out_shape=pltpu.VMEM((STN, 2, ROWS, ALL_INPUTS...  114 us
    convert_element_type x1, other arithmetic, per_device(): return vis.astype(F32)  4.46 us

profile of v2, /device:TPU:1, one launch (start us, length us, event | category | flops | bytes accessed | tf_op | source)
XLA Modules:
  0.0 118.7 jit_solution(5622217705863909833)
XLA Ops:
  0.0 114.2 %correlator.1 = bf16[8,2,128,1024]{3,2,1,0:T(8,128)(2,1)S(1)} custom-call(bf16[128,8192]{1,0:T(8,128)(2,1)} %volt_ref.1, f32[12,512]{1,0:T(8,128)} %taps_ref.1, bf16[2,2,256,256]{3,2,1,0:T(8,128)(2,1)} %constant.2.clone.table_ref), custom_call_target="tpu_custom_call" | custom-call | tf_op jit(solution)/shard_map/correlator/pallas_call | solution.py:329
  114.2 4.5 %convert_element_type.3 = f32[8,2,128,1024]{3,2,1,0:T(8,128)} convert(bf16[8,2,128,1024]{3,2,1,0:T(8,128)(2,1)S(1)} %correlator.1) | non-fusion elementwise | flops 2097152 | bytes 12582912 | tf_op jit(solution)/shard_map/convert_element_type | solution.py:354

commit v3 on v2

--- a/solution.py
+++ b/solution.py
@@ -31,7 +31,6 @@
 AFTER = QUAD
 BEFORE = HALO - AFTER
 SPAN = BEFORE + FRAMES + AFTER
-STN_STEPS = [(1, 0), (3, 0), (0, 1), (1, 1), (3, 1), (2, 0), (2, 1), (0, 0)]
 
 
 def dft_tables():
@@ -59,8 +58,8 @@
 
 
 def correlator(
-    volt_ref, taps_ref, table_ref, out_ref,
-    x_buf, tap_buf, fold_buf, wide_buf, send_buf, spec_buf, left_buf, vis_buf,
+    volt_ref, taps_any, table_any, out_ref,
+    taps_ref, table_ref, x_buf, tap_buf, fold_buf, wide_buf, send_buf, spec_buf, left_buf, vis_buf,
     local_sem, halo_send_sem, halo_recv_sem, spec_sem, vis_sem,
 ):
     tm = lax.axis_index("tm")
@@ -72,6 +71,10 @@
         volt_ref, x_buf.at[:, pl.ds(BEFORE * FRAME, FRAMES * FRAME)], local_sem.at[0]
     )
     own.start()
+    taps_copy = pltpu.make_async_copy(taps_any, taps_ref, local_sem.at[1])
+    taps_copy.start()
+    table_copy = pltpu.make_async_copy(table_any, table_ref, local_sem.at[2])
+    table_copy.start()
 
     barrier = pltpu.get_barrier_semaphore()
 
@@ -124,9 +127,11 @@
         halo_copy(2).start()
         start_before()
 
+    taps_copy.wait()
     for tap in range(TAPS):
         tap_buf[tap] = jnp.broadcast_to(taps_ref[tap : tap + 1, :], (16, FRAME))
     own.wait()
+    table_copy.wait()
 
     def fir(quad):
         base = quad * QUAD * FRAME
@@ -254,8 +259,6 @@
         left_buf[block, 1, :, ALL_FRAMES:] = -real
         return carry
 
-    lax.fori_loop(0, STN, left_step, 0)
-
     to_tm = (tm >> 1) * 2 + y_hi
     out_channel = x * 2 + 1 - core
 
@@ -264,34 +267,37 @@
         real = spec_buf[:, 0, :, at].reshape(ALL_FRAMES, COLS)
         imag = spec_buf[:, 1, :, at].reshape(ALL_FRAMES, COLS)
 
-        def block_step(step, inner):
-            blocks = pl.ds(step * BLOCKS, BLOCKS)
+        place = out_ref.at[out_channel, :, :, at]
+        for half in range(2):
+            first = ((stn >> 2) ^ 1 ^ half) * BLOCKS
+
+            @pl.when(col_step == 0)
+            def _():
+                lax.fori_loop(0, BLOCKS, lambda step, carry: left_step(first + step, carry), 0)
+
+            blocks = pl.ds(first, BLOCKS)
             left = left_buf[blocks].reshape(BLOCKS * 2 * ROWS, 2 * ALL_FRAMES)
             total = jnp.dot(left[:, :ALL_FRAMES], real, preferred_element_type=F32)
             total += jnp.dot(left[:, ALL_FRAMES:], imag, preferred_element_type=F32)
             total = (total * (1.0 / ALL_FRAMES)).astype(BF16)
             vis_buf[col_step, blocks] = total.reshape(BLOCKS, 2, ROWS, COLS)
-            return inner
-
-        lax.fori_loop(0, STN // BLOCKS, block_step, 0)
-        place = out_ref.at[out_channel, :, :, at]
-        for d_x, d_y in STN_STEPS:
-            to_stn = ((x + d_x) & 3) * 2 + (y_hi ^ d_y)
-
-            def start():
-                pltpu.make_async_remote_copy(
-                    src_ref=vis_buf.at[col_step, to_stn],
-                    dst_ref=place,
-                    send_sem=vis_sem.at[0],
-                    recv_sem=vis_sem.at[1],
-                    device_id=(to_tm, to_stn),
-                    device_id_type=MESH,
-                ).start()
-
-            if d_x or d_y:
-                start()
-            else:
-                pl.when(core != y_hi)(start)
+            for low in (2, 1, 3, 0):
+                to_stn = first + ((stn & 3) ^ low)
+
+                def start():
+                    pltpu.make_async_remote_copy(
+                        src_ref=vis_buf.at[col_step, to_stn],
+                        dst_ref=place,
+                        send_sem=vis_sem.at[0],
+                        recv_sem=vis_sem.at[1],
+                        device_id=(to_tm, to_stn),
+                        device_id_type=MESH,
+                    ).start()
+
+                if half == 0 or low:
+                    start()
+                else:
+                    pl.when(core != y_hi)(start)
 
         @pl.when(core == y_hi)
         def _():
@@ -325,13 +331,14 @@
 def per_device(voltages, fir_taps):
     tables = jnp.asarray(dft_tables())
     any_spec = pl.BlockSpec(memory_space=pl.ANY)
-    vmem_spec = pl.BlockSpec(memory_space=pltpu.VMEM)
     vis = pl.pallas_call(
         correlator,
         out_shape=pltpu.VMEM((STN, 2, ROWS, ALL_INPUTS), BF16),
-        in_specs=[any_spec, vmem_spec, vmem_spec],
+        in_specs=[any_spec, any_spec, any_spec],
         out_specs=any_spec,
         scratch_shapes=[
+            pltpu.VMEM((TAPS, FRAME), F32),
+            pltpu.VMEM((2, 2, 2 * SLOTS, HALF), BF16),
             pltpu.VMEM((ROWS, SPAN * FRAME), BF16),
             pltpu.VMEM((TAPS, 16, FRAME), F32),
             pltpu.VMEM((2, 2, FRAMES * ROWS, HALF), BF16),
@@ -340,7 +347,7 @@
             pltpu.VMEM((TM, 2, FRAMES, ALL_INPUTS), BF16),
             pltpu.VMEM((STN, 2, ROWS, 2 * ALL_FRAMES), BF16),
             pltpu.VMEM((COL_STEPS, STN, 2, ROWS, COLS), BF16),
-            pltpu.SemaphoreType.DMA((1,)),
+            pltpu.SemaphoreType.DMA((3,)),
             pltpu.SemaphoreType.DMA((3,)),
             pltpu.SemaphoreType.DMA((3,)),
             pltpu.SemaphoreType.DMA((2,)),

time: 119 us -> 119 us (level)
  no operation moved by 1% of the time
where the time goes in v3:
time: 119 us; the launch traced here: 118 us
  Pallas kernels  113 us (95%)
  other arithmetic  4.46 us (4%)
    pallas_call x1, Pallas kernels, per_device(): pl.pallas_call(correlator, out_shape=pltpu.VMEM((STN, 2, ROWS, ALL_INPUTS...  113 us
    convert_element_type x1, other arithmetic, per_device(): return vis.astype(F32)  4.46 us

profile of v3, /device:TPU:1, one launch (start us, length us, event | category | flops | bytes accessed | tf_op | source)
XLA Modules:
  0.0 117.7 jit_solution(2757412007181793688)
XLA Ops:
  0.0 113.2 %correlator.1 = bf16[8,2,128,1024]{3,2,1,0:T(8,128)(2,1)S(1)} custom-call(bf16[128,8192]{1,0:T(8,128)(2,1)} %volt_ref.1, f32[12,512]{1,0:T(8,128)} %taps_any.1, bf16[2,2,256,256]{3,2,1,0:T(8,128)(2,1)} %constant.2.clone.table_any), custom_call_target="tpu_custom_call" | custom-call | tf_op jit(solution)/shard_map/correlator/pallas_call | solution.py:334
  113.2 4.5 %convert_element_type.3 = f32[8,2,128,1024]{3,2,1,0:T(8,128)} convert(bf16[8,2,128,1024]{3,2,1,0:T(8,128)(2,1)S(1)} %correlator.1) | non-fusion elementwise | flops 2097152 | bytes 12582912 | tf_op jit(solution)/shard_map/convert_element_type | solution.py:361
